TPU v7x, 32 devices: a whole 2x2x4 slice. The times are simulated.
32 devices in a mesh: parts: 2 (over y), dp: 2 (over core), tensor: 8 (over z, x).
Axes of the slice: x: 2, y: 2, z: 4, core: 2. Of those that a mesh axis runs over, the one named last changes fastest.
Arguments:
- tokens: bfloat16 [4096, 6144], P(('parts', 'dp'), 'tensor'), parts along dimension 0, may hold values from -6 to 6
- expert_index: int32 [4096, 2], P(('parts', 'dp')), parts along dimension 0, may hold values from 0 to 7, as said below
- combine_weight: float32 [4096, 2], P(('parts', 'dp')), parts along dimension 0, may hold values from 0.2 to 1
- gate_weight: bfloat16 [6144, 16384], P(None, 'tensor'), may hold values from -0.078125 to 0.078125
- up_weight: bfloat16 [6144, 16384], P(None, 'tensor'), may hold values from -0.078125 to 0.078125
- down_weight: bfloat16 [16384, 6144], P('tensor'), may hold values from -0.0625 to 0.0625
Outputs:
- mixed: bfloat16 [4096, 6144], P(('parts', 'dp'), 'tensor'), parts along dimension 0
There are 2 independent parts, one for each index of `parts`. A program takes and returns all parts, laid end to end along the dimension named above; an argument that names none is the same for every part. Nothing has to cross between parts.
Inputs may be any that keep to these rules, and one draw needn't show every extreme that they name: `expert_index`: each row names 2 different experts. Among the tokens of one dp index (each aligned block of 1024 rows) at most 512 name expert 0, a quarter of 512 at least, and in every draw some block has exactly 512.
All inputs are finite; a program needn't handle non-finite values.
Results may differ from a plain program's by a relative error of at most 0.005.
Values may be sent and summed in bfloat16 or wider, within the bound.
No kernel may reach another device: no remote copies, remote signals or barrier semaphores. Data moves between devices by JAX's collectives and lax.ppermute only.
A program may use at most 192 MiB of HBM per device.

v0:
```python
import jax
import jax.numpy as jnp
from jax import lax
from jax.sharding import PartitionSpec as P

D = 6144
MOST = 512


def dispatch_table(index_block, weight_block):
    chosen = index_block == 0
    routed = jnp.any(chosen, axis=1)
    factor = jnp.sum(jnp.where(chosen, weight_block, 0.0), axis=1)
    position = jnp.cumsum(routed.astype(jnp.int32)) - 1
    slot_ids = jnp.arange(MOST, dtype=jnp.int32)
    select = (position[None, :] == slot_ids[:, None]) & routed[None, :]
    token_ids = jnp.arange(index_block.shape[0], dtype=jnp.int32)
    slot_token = jnp.sum(jnp.where(select, token_ids[None, :], 0), axis=1)
    slot_scale = jnp.sum(jnp.where(select, factor[None, :], 0.0), axis=1)
    return (slot_token, slot_scale)


def fold_columns(column_piece, gate_weight, up_weight):
    return (
        jnp.dot(column_piece, gate_weight, preferred_element_type=jnp.float32),
        jnp.dot(column_piece, up_weight, preferred_element_type=jnp.float32),
    )


def local(tokens, expert_index, combine_weight, gate_weight, up_weight, down_weight):
    token_count = tokens.shape[0]
    slot_token, slot_scale = dispatch_table(expert_index, combine_weight)
    selected = jnp.take(lax.all_gather(tokens, "tensor", axis=1, tiled=True), slot_token, axis=0)
    gate, up_part = fold_columns(selected, gate_weight, up_weight)
    hidden = (jax.nn.silu(gate) * up_part).astype(jnp.bfloat16)
    partial_value = (
        jnp.dot(hidden, down_weight, preferred_element_type=jnp.float32) * slot_scale[:, None]
    )
    spread = jnp.zeros((token_count, D), jnp.float32).at[slot_token].add(partial_value)
    mixed = lax.psum_scatter(spread, "tensor", scatter_dimension=1, tiled=True).astype(jnp.bfloat16)
    return mixed


def solution(mesh):
    in_specs = (
        P(("parts", "dp"), "tensor"),
        P(("parts", "dp"), None),
        P(("parts", "dp"), None),
        P(None, "tensor"),
        P(None, "tensor"),
        P("tensor", None),
    )
    out_specs = P(("parts", "dp"), "tensor")
    return jax.shard_map(local, mesh=mesh, in_specs=in_specs, out_specs=out_specs, check_vma=False)
```

profile of v0, /device:TPU:0, one launch (start us, length us, event | category | flops | bytes accessed | tf_op | source)
XLA Modules:
  0.0 714.7 jit_solution(2792084017324685766)
XLA Ops:
  6.5 0.0 all-gather.2.cloned.1.call-start
  6.5 0.7 all-gather.2.cloned.1.call-update
  7.3 0.0 reduce-scatter.2.cloned.1.call-start
  7.3 0.7 fusion.4
  8.0 0.3 reduce-window.9
  8.3 0.1 slice.7
  8.4 0.1 slice_reduce_fusion
  8.5 0.1 add_bitcast_fusion
  8.6 0.5 select_reduce_fusion.1
  9.1 0.7 select_reduce_fusion.2
  9.9 0.5 select_reduce_fusion
  10.4 178.1 %all-gather.2.cloned.1.call-done = bf16[1024,6144]{1,0:T(8,128)(2,1)} async-done(((bf16[1024,768]{1,0:T(8,128)(2,1)}), bf16[1024,6144]{1,0:T(8,128)(2,1)}) %all-gather.2.cloned.1.call-update) | async-done | bytes 12582928 | tf_op jit(solution)/shard_map/all_gather | solution.py:33
  188.5 18.5 %gather_fusion = bf16[512,6144]{1,0:T(8,128)(2,1)} fusion(bf16[1024,6144]{1,0:T(8,128)(2,1)} %all-gather.2.cloned.1.call-done, s32[1024]{0:T(1024)S(1)} %pad_clamp_fusion), kind=kCustom, calls=%fused_computation | custom fusion | bytes 12584960 | tf_op jit(solution)/shard_map/jit(_take)/gather | solution.py:33
  207.0 0.0 copy-start
  207.0 24.6 %fusion.2 = f32[512,2048]{1,0:T(8,128)} fusion(bf16[6144,2048]{1,0:T(8,128)(2,1)} %param.9, bf16[512,6144]{1,0:T(8,128)(2,1)} %gather_fusion, pred[512]{0:T(512)(128)(4,1)S(1)} %compare_and_fusion), kind=kOutput, calls=%fused_computation.7 | convolution fusion | flops 12888047616 | bytes 35652096 | tf_op jit(solution)/shard_map/dot_general | solution.py:25
  231.6 0.0 copy-done
  231.6 20.4 %multiply_convert_fusion = bf16[512,2048]{1,0:T(8,128)(2,1)} fusion(f32[512,2048]{1,0:T(8,128)} %fusion.2, bf16[6144,2048]{1,0:T(8,128)(2,1)} %param.10, bf16[512,6144]{1,0:T(8,128)(2,1)S(1)} %copy-done, pred[512]{0:T(512)(128)(4,1)S(1)} %compare_and_fusion), kind=kOutput, calls=%fused_computation.6 | convolution fusion | flops 12894339072 | bytes 37749248 | tf_op jit(solution)/shard_map/dot_general | solution.py:26
  252.0 21.1 %convolution_multiply_fusion = f32[512,6144]{1,0:T(8,128)} fusion(bf16[512,2048]{1,0:T(8,128)(2,1)} %multiply_convert_fusion, bf16[2048,6144]{1,0:T(8,128)(2,1)} %param.11, f32[512]{0:T(512)S(1)} %select_reduce_fusion), kind=kOutput, calls=%fused_computation.4 | convolution fusion | flops 12888047616 | bytes 39847936 | tf_op jit(solution)/shard_map/dot_general | solution.py:37
  273.1 29.2 %scatter_custom_fusion = f32[1024,6144]{1,0:T(8,128)} fusion(s32[512]{0:T(512)S(1)} %bitcast.11, f32[512,6144]{1,0:T(8,128)} %convolution_multiply_fusion, f32[]{:T(128)} %constant.11.clone.1), kind=kCustom, calls=%fused_computation.2 | custom fusion | flops 3145728 | bytes 25166336 | tf_op jit(solution)/shard_map/scatter-add | solution.py:39
  302.4 0.0 reduce-scatter.2.cloned.1.call-update
  302.4 402.1 %reduce-scatter.2.cloned.1.call-done = f32[1024,768]{1,0:T(8,128)} async-done(((f32[1024,6144]{1,0:T(8,128)}), f32[1024,768]{1,0:T(8,128)}) %reduce-scatter.2.cloned.1.call-update) | async-done | bytes 3145744 | tf_op jit(solution)/shard_map/reduce_scatter | solution.py:40
  704.5 3.2 convert_element_type.16
  (5 shorter events, 0.1 us)
Async XLA Ops:
  6.5 182.0 %all-gather.2.cloned.1.call-start = ((), (), s32[]{:S(2)}) async-start(), calls=%async_computation.1 | async-start | bytes 14155776 | tf_op jit(solution)/shard_map/all_gather | solution.py:33
  7.3 697.3 %reduce-scatter.2.cloned.1.call-start = ((), (), s32[]{:S(2)}) async-start(), calls=%async_computation.2 | async-start | bytes 28311552 | tf_op jit(solution)/shard_map/reduce_scatter | solution.py:40
  207.0 24.6 %copy-start = (bf16[512,6144]{1,0:T(8,128)(2,1)S(1)}, bf16[512,6144]{1,0:T(8,128)(2,1)}, u32[]{:S(2)}) copy-start(bf16[512,6144]{1,0:T(8,128)(2,1)} %gather_fusion) | copy-start | bytes 18874372
Sparse Core Ops, SparseCore 0:
  9.6 178.8 all-gather.1
  302.5 401.9 reduce-scatter.1
where the time goes:
time: 718 us; the launch traced here: 715 us
  waiting for transfers between devices  581 us (81%)
  matrix products  66.1 us (9%)
  other arithmetic  35.3 us (5%)
  local copies, waits for them, and re-layouts  18.7 us (3%)
  between operations  13.6 us (2%)
    reduce_scatter x1, waiting for transfers between devices, local(): lax.psum_scatter(spread, 'tensor', scatter_dimension=1, tiled=True)  402 us
    all_gather x1, waiting for transfers between devices, local(): lax.all_gather(tokens, 'tensor', axis=1, tiled=True)  178 us
    scatter-add x1, other arithmetic, local(): jnp.zeros((token_count, D), jnp.float32).at[slot_token].add(partial_value)  29.2 us
    dot_general x1, matrix products, fold_columns(): jnp.dot(column_piece, gate_weight, preferred_element_type=jnp.float32)  24.6 us
    dot_general x1, matrix products, local(): jnp.dot(hidden, down_weight, preferred_element_type=jnp.float32)  21.1 us
    dot_general x1, matrix products, fold_columns(): jnp.dot(column_piece, up_weight, preferred_element_type=jnp.float32)  20.4 us
    gather x1, local copies, waits for them, and re-layouts, local(): jnp.take(lax.all_gather(tokens, 'tensor', axis=1, tiled=True), slot_token...  18.5 us
  transfers between devices with their start and end apart: 2, of which 2 were waited for; matrix products, arithmetic and copies ran while one was open for 0% of the time, Pallas kernels for 0%

commit v1 on v0

v1 whole, which is shorter than its diff:
```python
import functools

import jax
import jax.numpy as jnp
from jax import lax
from jax.experimental import pallas as pl
from jax.experimental.pallas import tpu as pltpu
from jax.sharding import PartitionSpec as P

MOST = 512
LANES = 128
TILE = 256
F32 = jnp.float32
BF16 = jnp.bfloat16
VMEM_BYTES = 48 * 1024 * 1024


def params():
    return pltpu.CompilerParams(vmem_limit_bytes=VMEM_BYTES)


def dot(a, b):
    return jnp.dot(a, b, preferred_element_type=F32)


def compact_kernel(routed_ref, tokens_ref, chosen_ref, slot_ref, select_ref):
    slots = select_ref.shape[0]
    groups = routed_ref.shape[0]
    routed = routed_ref[...]
    above = lax.broadcasted_iota(jnp.int32, (LANES, LANES), 0) <= lax.broadcasted_iota(
        jnp.int32, (LANES, LANES), 1
    )
    within = dot(routed.astype(BF16), jnp.where(above, 1.0, 0.0).astype(BF16))
    before = jnp.zeros((1, 1), F32)
    slot_ids = lax.broadcasted_iota(jnp.int32, (slots, LANES), 0)
    for g in range(groups):
        row = within[g : g + 1, :] + before
        before = row[:, LANES - 1 :]
        slot = jnp.where(routed[g : g + 1, :] > 0, row.astype(jnp.int32) - 1, -1)
        slot_ref[g : g + 1, :] = slot
        select_ref[:, g * LANES : (g + 1) * LANES] = jnp.where(slot_ids == slot, 1.0, 0.0).astype(BF16)
    chosen_ref[...] = dot(select_ref[...], tokens_ref[...]).astype(BF16)


def compact(routed, tokens, slots):
    count, width = tokens.shape
    groups = count // LANES
    return pl.pallas_call(
        compact_kernel,
        out_shape=(
            jax.ShapeDtypeStruct((slots, width), BF16),
            jax.ShapeDtypeStruct((groups, LANES), jnp.int32),
        ),
        scratch_shapes=[pltpu.VMEM((slots, count), BF16)],
        compiler_params=params(),
        name="compact",
    )(routed.astype(F32).reshape(groups, LANES), tokens)


def gate_up_kernel(ids_ref, *refs, pieces, first, last):
    xs, refs = refs[:pieces], refs[pieces:]
    weights = 1 if last else pieces
    gates, refs = refs[:weights], refs[weights:]
    ups, refs = refs[:weights], refs[weights:]
    if last:
        gate_in, up_in, hidden_ref = refs
        rows = xs[0].shape[0]
        for half in range(2):
            at = slice(half * rows, (half + 1) * rows)
            gate = gate_in[at, :] + dot(xs[half][...], gates[0][...])
            up = up_in[at, :] + dot(xs[half][...], ups[0][...])
            hidden_ref[at, :] = (gate / (1.0 + jnp.exp(-gate)) * up).astype(BF16)
        return
    gate = dot(xs[0][...], gates[0][...])
    up = dot(xs[0][...], ups[0][...])
    for i in range(1, pieces):
        gate += dot(xs[i][...], gates[i][...])
        up += dot(xs[i][...], ups[i][...])
    if first:
        gate_out, up_out = refs
        gate_out[...] = gate
        up_out[...] = up
    else:
        gate_in, up_in, gate_out, up_out = refs
        gate_out[...] = gate_in[...] + gate
        up_out[...] = up_in[...] + up


def gate_up(ids, steps, xs, gate_weight, up_weight, sums, last=False):
    width = xs[0].shape[1]
    hidden = gate_weight.shape[1]
    slots = xs[0].shape[0] * (2 if last else 1)
    first = sums is None
    weights = [
        pl.BlockSpec((width, TILE), functools.partial(lambda n, ids, j: (ids[j], n), j=j))
        for j in steps
    ]
    block = pl.BlockSpec((slots, TILE), lambda n, ids: (0, n))
    xspecs = [pl.BlockSpec(x.shape, lambda n, ids: (0, 0)) for x in xs]
    total = jax.ShapeDtypeStruct((slots, hidden), F32)
    in_specs = xspecs + weights + weights + ([] if first else [block, block])
    operands = [*xs, *[gate_weight] * len(steps), *[up_weight] * len(steps), *([] if first else sums)]
    aliases = {}
    if last:
        out_shape, out_specs = jax.ShapeDtypeStruct((slots, hidden), BF16), block
    else:
        out_shape, out_specs = (total, total), (block, block)
        if not first:
            at = 1 + len(operands) - 2
            aliases = {at: 0, at + 1: 1}
    flops = 4 * slots * width * hidden * len(steps)
    moved = 4 * width * hidden * len(steps) + 16 * slots * hidden
    return pl.pallas_call(
        functools.partial(gate_up_kernel, pieces=len(xs), first=first, last=last),
        grid_spec=pltpu.PrefetchScalarGridSpec(
            num_scalar_prefetch=1, grid=(hidden // TILE,), in_specs=in_specs, out_specs=out_specs
        ),
        out_shape=out_shape,
        input_output_aliases=aliases,
        compiler_params=params(),
        cost_estimate=pl.CostEstimate(flops=flops, bytes_accessed=moved, transcendentals=0),
        name="gate_up",
    )(ids, *operands)


def down_kernel(ids_ref, hidden_ref, *refs, pieces, split):
    weights, outs = refs[:pieces], refs[pieces:]
    hidden = hidden_ref[...]
    for i in range(pieces):
        value = dot(hidden, weights[i][...])
        if split:
            rows = outs[0].shape[0]
            outs[0][...] = value[:rows].astype(BF16)
            outs[1][...] = value[rows:].astype(BF16)
        else:
            outs[i][...] = value


def down(ids, steps, hidden, down_weight, width, split=False):
    slots, depth = hidden.shape
    tiles = width // TILE
    weights = [
        pl.BlockSpec((depth, TILE), functools.partial(lambda n, ids, j: (0, ids[j] * tiles + n), j=j))
        for j in steps
    ]
    if split:
        shape, kind, outs = (slots // 2, width), BF16, 2
    else:
        shape, kind, outs = (slots, width), F32, len(steps)
    return pl.pallas_call(
        functools.partial(down_kernel, pieces=len(steps), split=split),
        grid_spec=pltpu.PrefetchScalarGridSpec(
            num_scalar_prefetch=1,
            grid=(tiles,),
            in_specs=[pl.BlockSpec(hidden.shape, lambda n, ids: (0, 0))] + weights,
            out_specs=(pl.BlockSpec((shape[0], TILE), lambda n, ids: (0, n)),) * outs,
        ),
        out_shape=(jax.ShapeDtypeStruct(shape, kind),) * outs,
        compiler_params=params(),
        cost_estimate=pl.CostEstimate(
            flops=2 * slots * depth * width * len(steps),
            bytes_accessed=2 * depth * width * len(steps) + 4 * slots * width * len(steps),
            transcendentals=0,
        ),
        name="down",
    )(ids, hidden, *[down_weight] * len(steps))


def spread_kernel(place_ref, scale_ref, own_ref, right_ref, left_ref, out_ref):
    total = own_ref[...] + right_ref[...].astype(F32) + left_ref[...].astype(F32)
    scaled = (total * scale_ref[...]).astype(BF16)
    out_ref[...] = dot(place_ref[...], scaled).astype(BF16)


def spread(place, scale, own, right, left):
    count, slots = place.shape
    width = own.shape[1]
    block = pl.BlockSpec((slots, TILE), lambda n: (0, n))
    return pl.pallas_call(
        spread_kernel,
        grid=(width // TILE,),
        in_specs=[
            pl.BlockSpec(place.shape, lambda n: (0, 0)),
            pl.BlockSpec(scale.shape, lambda n: (0, 0)),
            block,
            block,
            block,
        ],
        out_specs=pl.BlockSpec((count, TILE), lambda n: (0, n)),
        out_shape=jax.ShapeDtypeStruct((count, width), BF16),
        compiler_params=params(),
        name="spread",
    )(place, scale, own, right, left)


def ring_of(size):
    return [*range(0, size, 2), *range(size - 1, 0, -2)]


def ring_plan(size, slots, tokens, routed, factor, gate_weight, up_weight, down_weight):
    width = tokens.shape[1]
    half = size // 2
    order = ring_of(size)
    table = [[order[(order.index(me) + s) % size] for s in range(size)] for me in range(size)]
    ids = jnp.asarray(table, jnp.int32)[lax.axis_index("tensor")]
    to_right = [(order[i], order[(i + 1) % size]) for i in range(size)]
    to_left = [(b, a) for a, b in to_right]

    def right_of(value):
        return lax.ppermute(value, "tensor", to_right)

    def left_of(value):
        return lax.ppermute(value, "tensor", to_left)

    own, slot = compact(routed, tokens, slots)

    right, left = right_of(own), left_of(own)
    sums = gate_up(ids, [0], [own], gate_weight, up_weight, None)
    for s in range(1, half):
        here = [right, left]
        if s + 1 < half:
            right, left = right_of(right), left_of(left)
        else:
            right, left = right_of(right[: slots // 2]), left_of(left[slots // 2 :])
        sums = gate_up(ids, [size - s, s], here, gate_weight, up_weight, sums)
    hidden = gate_up(ids, [half], [right, left], gate_weight, up_weight, sums, last=True)

    top, bottom = down(ids, [half], hidden, down_weight, width, split=True)
    right, left = right_of(top), left_of(bottom)
    for s in range(half - 1, 0, -1):
        ahead, behind = down(ids, [s, size - s], hidden, down_weight, width)
        if s == half - 1:
            rows = slots // 2
            ahead = jnp.concatenate([ahead[:rows] + right.astype(F32), ahead[rows:]])
            behind = jnp.concatenate([behind[:rows], behind[rows:] + left.astype(F32)])
        else:
            ahead = ahead + right.astype(F32)
            behind = behind + left.astype(F32)
        right, left = right_of(ahead.astype(BF16)), left_of(behind.astype(BF16))
    (mine,) = down(ids, [0], hidden, down_weight, width)

    slot = slot.reshape(-1)
    slot_ids = jnp.arange(slots, dtype=jnp.int32)
    place = (slot[:, None] == slot_ids[None, :]).astype(BF16)
    scale = jnp.sum(jnp.where(slot_ids[:, None] == slot[None, :], factor[None, :], 0.0), axis=1)
    return spread(place, scale[:, None], mine, right, left)


def plain_plan(slots, tokens, routed, factor, gate_weight, up_weight, down_weight):
    slot = jnp.where(routed, jnp.cumsum(routed.astype(jnp.int32)) - 1, -1)
    slot_ids = jnp.arange(slots, dtype=jnp.int32)
    select = slot_ids[:, None] == slot[None, :]
    chosen = dot(select.astype(BF16), tokens).astype(BF16)
    scale = jnp.sum(jnp.where(select, factor[None, :], 0.0), axis=1)
    full = lax.all_gather(chosen, "tensor", axis=1, tiled=True)
    gate, up = dot(full, gate_weight), dot(full, up_weight)
    hidden = (jax.nn.silu(gate) * up).astype(BF16)
    partial = dot(hidden, down_weight) * scale[:, None]
    total = lax.psum_scatter(partial, "tensor", scatter_dimension=1, tiled=True)
    return dot(select.T.astype(BF16), total.astype(BF16)).astype(BF16)


def local(size, tokens, expert_index, combine_weight, gate_weight, up_weight, down_weight):
    chosen = expert_index == 0
    routed = jnp.any(chosen, axis=1)
    factor = jnp.sum(jnp.where(chosen, combine_weight, 0.0), axis=1)
    rest = (tokens, routed, factor, gate_weight, up_weight, down_weight)
    fits = (
        size >= 4
        and size % 2 == 0
        and tokens.shape[1] % TILE == 0
        and gate_weight.shape[1] % TILE == 0
        and tokens.shape[0] % LANES == 0
    )
    if fits:
        return ring_plan(size, MOST, *rest)
    return plain_plan(MOST, *rest)


def solution(mesh):
    rows = P(("parts", "dp"), "tensor")
    in_specs = (
        rows,
        P(("parts", "dp"), None),
        P(("parts", "dp"), None),
        P(None, "tensor"),
        P(None, "tensor"),
        P("tensor", None),
    )
    return jax.shard_map(
        functools.partial(local, mesh.shape["tensor"]),
        mesh=mesh,
        in_specs=in_specs,
        out_specs=rows,
        check_vma=False,
    )
```

time: 718 us -> 176 us (0.25)
  waiting for transfers between devices: 581 us -> 53.7 us
  Pallas kernels: 0 us -> 94 us
  matrix products: 66.1 us -> 0 us
  other arithmetic: 35.3 us -> 3.99 us
  starting transfers between devices: 0.04 us -> 16.6 us
  between operations: 13.6 us -> 0.15 us
  local copies, waits for them, and re-layouts: 18.7 us -> 6.4 us
    reduce_scatter x1 -> x0, waiting for transfers between devices: 402 us -> none  [local(): lax.psum_scatter(spread, 'tensor', scatter_dimension=1, tiled=True)]
    all_gather x1 -> x0, waiting for transfers between devices: 178 us -> none  [local(): lax.all_gather(tokens, 'tensor', axis=1, tiled=True)]
    pallas_call x0 -> x12, Pallas kernels: none -> 94 us  [the longest x5 60.7 us: gate_up(): pl.pallas_call(functools.partial(gate_up_kernel, pieces=len(xs), first=fi...]
    dot_general x3 -> x0, matrix products: 66.1 us -> none  [the longest x1 24.6 us: fold_columns(): jnp.dot(column_piece, gate_weight, preferred_element_type=jnp.float32)]
    ppermute x0 -> x16, waiting for transfers between devices: none -> 53.7 us  [the longest x8 49.9 us: right_of(): return lax.ppermute(value, 'tensor', to_right)]
    scatter-add x1 -> x0, other arithmetic: 29.2 us -> none  [local(): jnp.zeros((token_count, D), jnp.float32).at[slot_token].add(partial_value)]
    gather x1 -> x0, local copies, waits for them, and re-layouts: 18.5 us -> none  [local(): jnp.take(lax.all_gather(tokens, 'tensor', axis=1, tiled=True), slot_token...]
    ppermute x0 -> x16, starting transfers between devices: none -> 16.6 us  [the longest x8 9.52 us: right_of(): return lax.ppermute(value, 'tensor', to_right)]
  transfers between devices with their start and end apart: 2 -> 16, of which waited for: 2 -> 9; matrix products, arithmetic and copies ran while one was open for 0% -> 2% of each run, Pallas kernels for 0% -> 42%
where the time goes in v1:
time: 176 us; the launch traced here: 175 us
  Pallas kernels  94 us (53%)
  waiting for transfers between devices  53.7 us (31%)
  starting transfers between devices  16.6 us (9%)
  local copies, waits for them, and re-layouts  6.4 us (4%)
  other arithmetic  3.99 us (2%)
    pallas_call x5, Pallas kernels, gate_up(): pl.pallas_call(functools.partial(gate_up_kernel, pieces=len(xs), first=fi...  60.7 us
    ppermute x8, waiting for transfers between devices, right_of(): return lax.ppermute(value, 'tensor', to_right)  49.9 us
    pallas_call x5, Pallas kernels, down(): pl.pallas_call(functools.partial(down_kernel, pieces=len(steps), split=sp...  27.9 us
    ppermute x8, starting transfers between devices, right_of(): return lax.ppermute(value, 'tensor', to_right)  9.52 us
    ppermute x8, starting transfers between devices, left_of(): return lax.ppermute(value, 'tensor', to_left)  7.11 us
    unnamed x12, local copies, waits for them, and re-layouts  5.42 us
    pallas_call x1, Pallas kernels, spread(): pl.pallas_call(spread_kernel, grid=(width // TILE,), in_specs=[pl.BlockSp...  4.01 us
    ppermute x8, waiting for transfers between devices, left_of(): return lax.ppermute(value, 'tensor', to_left)  3.83 us
  transfers between devices with their start and end apart: 16, of which 9 were waited for; matrix products, arithmetic and copies ran while one was open for 2% of the time, Pallas kernels for 42%

profile of v1, /device:TPU:0, one launch (start us, length us, event | category | flops | bytes accessed | tf_op | source)
XLA Modules:
  0.0 174.9 jit_solution(4505240029830985973)
XLA Ops:
  0.0 0.7 fusion.1
  0.7 1.4 copy-done.1
  2.1 1.4 compact.1
  3.5 3.1 %collective-permute-start = (bf16[512,768]{1,0:T(8,128)(2,1)S(1)}, bf16[512,768]{1,0:T(8,128)(2,1)S(1)}, u32[]{:S(2)}, u32[]{:S(2)}) collective-permute-start(bf16[512,768]{1,0:T(8,128)(2,1)S(1)} %get-tuple-element.24.refs_0_), channel_id=1, source_target_pairs={{0,2},{2,4},{4,6},{6,7},{7,5},{5,3},{3,1},{1,0},{8,10},{10,12},{12... | collective-permute-start | bytes 2359304 | tf_op jit(solution)/shard_map/ppermute | solution.py:210
  6.6 0.9 copy-done.2
  7.5 16.6 %collective-permute-done.refs_0_ = bf16[512,768]{1,0:T(8,128)(2,1)S(1)} collective-permute-done((bf16[512,768]{1,0:T(8,128)(2,1)S(1)}, bf16[512,768]{1,0:T(8,128)(2,1)S(1)}, u32[]{:S(2)}, u32[]{:S(2)}) %collective-permute-start) | collective-permute-done | bytes 786464 | tf_op jit(solution)/shard_map/ppermute | solution.py:210
  24.0 1.8 %collective-permute-start.1 = (bf16[512,768]{1,0:T(8,128)(2,1)S(1)}, bf16[512,768]{1,0:T(8,128)(2,1)S(1)}, u32[]{:S(2)}, u32[]{:S(2)}) collective-permute-start(bf16[512,768]{1,0:T(8,128)(2,1)S(1)} %collective-permute-done.refs_0_), channel_id=1, source_target_pairs={{0,2},{2,4},{4,6},{6,7},{7,5},{5,3},{3,1},{1,0},{8,10},{10,12},{12... | collective-permute-start | bytes 2359304 | tf_op jit(solution)/shard_map/ppermute | solution.py:210
  25.9 0.2 collective-permute-start.5
  26.1 0.7 dynamic-slice_bitcast_fusion.ids_ref
  26.8 1.1 copy-done.3
  27.9 9.6 %gate_up.5 = (f32[512,2048]{1,0:T(8,128)S(1)}, f32[512,2048]{1,0:T(8,128)}) custom-call(s32[8]{0:T(128)S(1)} %dynamic-slice_bitcast_fusion.ids_ref, bf16[512,768]{1,0:T(8,128)(2,1)S(1)} %copy-done.3, bf16[6144,2048]{1,0:T(8,128)(2,1)} %refs_2_.9, bf16[6144,2048]{1,0:T(8,128)(2,1)} %refs_3_.7), custom_call_target="tpu_custom_call" | custom-call | flops 3221225472 | bytes 23068672 | tf_op jit(solution)/shard_map/gate_up/pallas_call | solution.py:113
  37.5 5.2 %collective-permute-done.1.refs_0_ = bf16[512,768]{1,0:T(8,128)(2,1)S(1)} collective-permute-done((bf16[512,768]{1,0:T(8,128)(2,1)S(1)}, bf16[512,768]{1,0:T(8,128)(2,1)S(1)}, u32[]{:S(2)}, u32[]{:S(2)}) %collective-permute-start.1) | collective-permute-done | bytes 786464 | tf_op jit(solution)/shard_map/ppermute | solution.py:210
  42.8 1.5 collective-permute-start.2
  44.3 0.5 collective-permute-start.6
  44.8 13.7 %gate_up.6 = (f32[512,2048]{1,0:T(8,128)S(1)}, f32[512,2048]{1,0:T(8,128)}) custom-call(s32[8]{0:T(128)S(1)} %dynamic-slice_bitcast_fusion.ids_ref, bf16[512,768]{1,0:T(8,128)(2,1)S(1)} %collective-permute-done.refs_0_, bf16[512,768]{1,0:T(8,128)(2,1)S(1)} %collective-permute-done.4.refs_1_, ...), custom_call_target="tpu_custom_call", output_to_operand_aliasing={{0}: (7, {}), {1}: (8, {})} | custom-call | flops 6442450944 | bytes 29360128 | tf_op jit(solution)/shard_map/gate_up/pallas_call | solution.py:113
  58.5 13.7 %gate_up.7 = (f32[512,2048]{1,0:T(8,128)S(1)}, f32[512,2048]{1,0:T(8,128)}) custom-call(s32[8]{0:T(128)S(1)} %dynamic-slice_bitcast_fusion.ids_ref, bf16[512,768]{1,0:T(8,128)(2,1)S(1)} %collective-permute-done.1.refs_0_, bf16[512,768]{1,0:T(8,128)(2,1)S(1)} %collective-permute-done.5.refs_1_, ...), custom_call_target="tpu_custom_call", output_to_operand_aliasing={{0}: (7, {}), {1}: (8, {})} | custom-call | flops 6442450944 | bytes 29360128 | tf_op jit(solution)/shard_map/gate_up/pallas_call | solution.py:113
  72.2 1.6 collective-permute-start.3
  73.8 0.6 collective-permute-start.7
  74.4 13.7 %gate_up.8 = (f32[512,2048]{1,0:T(8,128)S(1)}, f32[512,2048]{1,0:T(8,128)}) custom-call(s32[8]{0:T(128)S(1)} %dynamic-slice_bitcast_fusion.ids_ref, bf16[512,768]{1,0:T(8,128)(2,1)S(1)} %collective-permute-done.2.refs_0_, bf16[512,768]{1,0:T(8,128)(2,1)S(1)} %collective-permute-done.6.refs_1_, ...), custom_call_target="tpu_custom_call", output_to_operand_aliasing={{0}: (7, {}), {1}: (8, {})} | custom-call | flops 6442450944 | bytes 29360128 | tf_op jit(solution)/shard_map/gate_up/pallas_call | solution.py:113
  88.1 2.0 %copy-done = f32[512,2048]{1,0:T(8,128)} copy-done((f32[512,2048]{1,0:T(8,128)}, f32[512,2048]{1,0:T(8,128)S(1)}, u32[]{:S(2)}) %copy-start) | copy-done | bytes 4194328
  90.1 10.0 %gate_up.9.hidden_ref = bf16[512,2048]{1,0:T(8,128)(2,1)S(1)} custom-call(s32[8]{0:T(128)S(1)} %dynamic-slice_bitcast_fusion.ids_ref, bf16[256,768]{1,0:T(8,128)(2,1)S(1)} %collective-permute-done.3.refs_0_, bf16[256,768]{1,0:T(8,128)(2,1)S(1)} %collective-permute-done.7.refs_1_, bf16[6144,2048]{1,0:T(8,128)(2,1)} %refs_2_.9, bf16[6144,2048]{1,0:T(8,128)(2,1)} %refs_3_.7, ...), custom_call_target="tpu_custom_call" | custom-call | flops 3221225472 | bytes 23068672 | tf_op jit(solution)/shard_map/gate_up/pallas_call | solution.py:113
  100.1 4.5 %down.9 = (bf16[256,768]{1,0:T(8,128)(2,1)S(1)}, bf16[256,768]{1,0:T(8,128)(2,1)S(1)}) custom-call(s32[8]{0:T(128)S(1)} %dynamic-slice_bitcast_fusion.ids_ref, bf16[512,2048]{1,0:T(8,128)(2,1)S(1)} %gate_up.9.hidden_ref, bf16[2048,6144]{1,0:T(8,128)(2,1)} %refs_0_.9), custom_call_target="tpu_custom_call" | custom-call | flops 1610612736 | bytes 4718592 | tf_op jit(solution)/shard_map/down/pallas_call | solution.py:150
  104.6 1.5 collective-permute-start.12
  106.0 6.3 %down.8 = (f32[512,768]{1,0:T(8,128)S(1)}, f32[512,768]{1,0:T(8,128)S(1)}) custom-call(s32[8]{0:T(128)S(1)} %dynamic-slice_bitcast_fusion.ids_ref, bf16[512,2048]{1,0:T(8,128)(2,1)S(1)} %gate_up.9.hidden_ref, bf16[2048,6144]{1,0:T(8,128)(2,1)} %refs_0_.9, bf16[2048,6144]{1,0:T(8,128)(2,1)} %refs_0_.9), custom_call_target="tpu_custom_call" | custom-call | flops 3221225472 | bytes 9437184 | tf_op jit(solution)/shard_map/down/pallas_call | solution.py:150
  112.4 0.7 collective-permute-start.8
  113.3 1.5 collective-permute-start.13
  114.7 7.2 %collective-permute-done.8 = bf16[256,768]{1,0:T(8,128)(2,1)S(1)} collective-permute-done((bf16[256,768]{1,0:T(8,128)(2,1)S(1)}, bf16[256,768]{1,0:T(8,128)(2,1)S(1)}, u32[]{:S(2)}, u32[]{:S(2)}) %collective-permute-start.8) | collective-permute-done | bytes 393248 | tf_op jit(solution)/shard_map/ppermute | solution.py:210
  122.0 0.3 collective-permute-start.9
  122.4 6.3 %down.7 = (f32[512,768]{1,0:T(8,128)S(1)}, f32[512,768]{1,0:T(8,128)S(1)}) custom-call(s32[8]{0:T(128)S(1)} %dynamic-slice_bitcast_fusion.ids_ref, bf16[512,2048]{1,0:T(8,128)(2,1)S(1)} %gate_up.9.hidden_ref, bf16[2048,6144]{1,0:T(8,128)(2,1)} %refs_0_.9, bf16[2048,6144]{1,0:T(8,128)(2,1)} %refs_0_.9), custom_call_target="tpu_custom_call" | custom-call | flops 3221225472 | bytes 9437184 | tf_op jit(solution)/shard_map/down/pallas_call | solution.py:150
  128.7 2.1 %collective-permute-done.13 = bf16[512,768]{1,0:T(8,128)(2,1)S(1)} collective-permute-done((bf16[512,768]{1,0:T(8,128)(2,1)S(1)}, bf16[512,768]{1,0:T(8,128)(2,1)S(1)}, u32[]{:S(2)}, u32[]{:S(2)}) %collective-permute-start.13) | collective-permute-done | bytes 786464 | tf_op jit(solution)/shard_map/ppermute | solution.py:213
  130.8 0.2 add_convert_fusion.1
  131.0 1.5 collective-permute-start.14
  132.5 7.1 %collective-permute-done.9 = bf16[512,768]{1,0:T(8,128)(2,1)S(1)} collective-permute-done((bf16[512,768]{1,0:T(8,128)(2,1)S(1)}, bf16[512,768]{1,0:T(8,128)(2,1)S(1)}, u32[]{:S(2)}, u32[]{:S(2)}) %collective-permute-start.9) | collective-permute-done | bytes 786464 | tf_op jit(solution)/shard_map/ppermute | solution.py:210
  139.6 0.2 add_convert_fusion.3
  139.8 0.3 collective-permute-start.10
  140.1 6.3 %down.6 = (f32[512,768]{1,0:T(8,128)S(1)}, f32[512,768]{1,0:T(8,128)S(1)}) custom-call(s32[8]{0:T(128)S(1)} %dynamic-slice_bitcast_fusion.ids_ref, bf16[512,2048]{1,0:T(8,128)(2,1)S(1)} %gate_up.9.hidden_ref, bf16[2048,6144]{1,0:T(8,128)(2,1)} %refs_0_.9, bf16[2048,6144]{1,0:T(8,128)(2,1)} %refs_0_.9), custom_call_target="tpu_custom_call" | custom-call | flops 3221225472 | bytes 9437184 | tf_op jit(solution)/shard_map/down/pallas_call | solution.py:150
  146.4 1.1 collective-permute-done.14
  147.5 1.1 add_convert_fusion
  148.5 1.4 collective-permute-start.15
  150.0 6.3 %collective-permute-done.10 = bf16[512,768]{1,0:T(8,128)(2,1)S(1)} collective-permute-done((bf16[512,768]{1,0:T(8,128)(2,1)S(1)}, bf16[512,768]{1,0:T(8,128)(2,1)S(1)}, u32[]{:S(2)}, u32[]{:S(2)}) %collective-permute-start.10) | collective-permute-done | bytes 786464 | tf_op jit(solution)/shard_map/ppermute | solution.py:210
  156.3 1.0 add_convert_fusion.2
  157.3 0.3 collective-permute-start.11
  157.6 0.3 select_reduce_fusion
  158.0 0.2 fusion.place_ref
  158.3 4.5 %down.5.own_ref = f32[512,768]{1,0:T(8,128)S(1)} custom-call(s32[8]{0:T(128)S(1)} %dynamic-slice_bitcast_fusion.ids_ref, bf16[512,2048]{1,0:T(8,128)(2,1)S(1)} %gate_up.9.hidden_ref, bf16[2048,6144]{1,0:T(8,128)(2,1)} %refs_0_.9), custom_call_target="tpu_custom_call" | custom-call | flops 1610612736 | bytes 4718592 | tf_op jit(solution)/shard_map/down/pallas_call | solution.py:150
  162.8 0.6 collective-permute-done.15.left_ref
  163.4 7.5 %collective-permute-done.11.right_ref = bf16[512,768]{1,0:T(8,128)(2,1)} collective-permute-done((bf16[512,768]{1,0:T(8,128)(2,1)}, bf16[512,768]{1,0:T(8,128)(2,1)}, u32[]{:S(2)}, u32[]{:S(2)}) %collective-permute-start.11) | collective-permute-done | bytes 786464 | tf_op jit(solution)/shard_map/ppermute | solution.py:210
  170.9 4.0 %spread.1 = bf16[1024,768]{1,0:T(8,128)(2,1)} custom-call(bf16[1024,512]{1,0:T(8,128)(2,1)S(1)} %fusion.place_ref, f32[512,1]{1,0:T(8,128)S(1)} %copy.15.scale_ref, f32[512,768]{1,0:T(8,128)S(1)} %down.5.own_ref, bf16[512,768]{1,0:T(8,128)(2,1)} %collective-permute-done.11.right_ref, bf16[512,768]{1,0:T(8,128)(2,1)S(1)} %collective-permute-done.15.left_ref), custom_call_target="tpu_custom_call" | custom-call | tf_op jit(solution)/shard_map/spread/pallas_call | solution.py:179
  (27 shorter events, 0.6 us)
Async XLA Ops:
  0.7 1.4 copy-start.1
  3.5 20.5 %collective-permute-start = (bf16[512,768]{1,0:T(8,128)(2,1)S(1)}, bf16[512,768]{1,0:T(8,128)(2,1)S(1)}, u32[]{:S(2)}, u32[]{:S(2)}) collective-permute-start(bf16[512,768]{1,0:T(8,128)(2,1)S(1)} %get-tuple-element.24.refs_0_), channel_id=1, source_target_pairs={{0,2},{2,4},{4,6},{6,7},{7,5},{5,3},{3,1},{1,0},{8,10},{10,12},{12... | collective-permute-start | bytes 2359304 | tf_op jit(solution)/shard_map/ppermute | solution.py:210
  6.6 19.3 %collective-permute-start.4 = (bf16[512,768]{1,0:T(8,128)(2,1)S(1)}, bf16[512,768]{1,0:T(8,128)(2,1)S(1)}, u32[]{:S(2)}, u32[]{:S(2)}) collective-permute-start(bf16[512,768]{1,0:T(8,128)(2,1)S(1)} %get-tuple-element.24.refs_0_), channel_id=1, source_target_pairs={{2,0},{4,2},{6,4},{7,6},{5,7},{3,5},{1,3},{0,1},{10,8},{12,10},{14... | collective-permute-start | bytes 2359304 | tf_op jit(solution)/shard_map/ppermute | solution.py:213
  6.6 0.9 copy-start.2
  24.0 18.7 %collective-permute-start.1 = (bf16[512,768]{1,0:T(8,128)(2,1)S(1)}, bf16[512,768]{1,0:T(8,128)(2,1)S(1)}, u32[]{:S(2)}, u32[]{:S(2)}) collective-permute-start(bf16[512,768]{1,0:T(8,128)(2,1)S(1)} %collective-permute-done.refs_0_), channel_id=1, source_target_pairs={{0,2},{2,4},{4,6},{6,7},{7,5},{5,3},{3,1},{1,0},{8,10},{10,12},{12... | collective-permute-start | bytes 2359304 | tf_op jit(solution)/shard_map/ppermute | solution.py:210
  25.9 18.4 %collective-permute-start.5 = (bf16[512,768]{1,0:T(8,128)(2,1)S(1)}, bf16[512,768]{1,0:T(8,128)(2,1)S(1)}, u32[]{:S(2)}, u32[]{:S(2)}) collective-permute-start(bf16[512,768]{1,0:T(8,128)(2,1)S(1)} %collective-permute-done.4.refs_1_), channel_id=1, source_target_pairs={{2,0},{4,2},{6,4},{7,6},{5,7},{3,5},{1,3},{0,1},{10,8},{12,10},{14... | collective-permute-start | bytes 2359304 | tf_op jit(solution)/shard_map/ppermute | solution.py:213
  26.8 1.1 copy-start.3
  42.8 29.4 %collective-permute-start.2 = (bf16[512,768]{1,0:T(8,128)(2,1)S(1)}, bf16[512,768]{1,0:T(8,128)(2,1)S(1)}, u32[]{:S(2)}, u32[]{:S(2)}) collective-permute-start(bf16[512,768]{1,0:T(8,128)(2,1)S(1)} %collective-permute-done.1.refs_0_), channel_id=1, source_target_pairs={{0,2},{2,4},{4,6},{6,7},{7,5},{5,3},{3,1},{1,0},{8,10},{10,12},{12... | collective-permute-start | bytes 2359304 | tf_op jit(solution)/shard_map/ppermute | solution.py:210
  44.3 29.5 %collective-permute-start.6 = (bf16[512,768]{1,0:T(8,128)(2,1)S(1)}, bf16[512,768]{1,0:T(8,128)(2,1)S(1)}, u32[]{:S(2)}, u32[]{:S(2)}) collective-permute-start(bf16[512,768]{1,0:T(8,128)(2,1)S(1)} %collective-permute-done.5.refs_1_), channel_id=1, source_target_pairs={{2,0},{4,2},{6,4},{7,6},{5,7},{3,5},{1,3},{0,1},{10,8},{12,10},{14... | collective-permute-start | bytes 2359304 | tf_op jit(solution)/shard_map/ppermute | solution.py:213
  72.2 17.9 %collective-permute-start.3 = (bf16[256,768]{1,0:T(8,128)(2,1)S(1)}, bf16[256,768]{1,0:T(8,128)(2,1)S(1)}, u32[]{:S(2)}, u32[]{:S(2)}) collective-permute-start(bf16[256,768]{1,0:T(8,128)(2,1)S(1)} %slice.26), channel_id=1, source_target_pairs={{0,2},{2,4},{4,6},{6,7},{7,5},{5,3},{3,1},{1,0},{8,10},{10,12},{12... | collective-permute-start | bytes 1179656 | tf_op jit(solution)/shard_map/ppermute | solution.py:210
  73.8 16.3 %collective-permute-start.7 = (bf16[256,768]{1,0:T(8,128)(2,1)S(1)}, bf16[256,768]{1,0:T(8,128)(2,1)S(1)}, u32[]{:S(2)}, u32[]{:S(2)}) collective-permute-start(bf16[256,768]{1,0:T(8,128)(2,1)S(1)} %slice.27), channel_id=1, source_target_pairs={{2,0},{4,2},{6,4},{7,6},{5,7},{3,5},{1,3},{0,1},{10,8},{12,10},{14... | collective-permute-start | bytes 1179656 | tf_op jit(solution)/shard_map/ppermute | solution.py:213
  88.1 2.0 %copy-start = (f32[512,2048]{1,0:T(8,128)}, f32[512,2048]{1,0:T(8,128)S(1)}, u32[]{:S(2)}) copy-start(f32[512,2048]{1,0:T(8,128)S(1)} %get-tuple-element.31.refs_4_) | copy-start | bytes 12582916
  104.6 8.6 %collective-permute-start.12 = (bf16[256,768]{1,0:T(8,128)(2,1)S(1)}, bf16[256,768]{1,0:T(8,128)(2,1)S(1)}, u32[]{:S(2)}, u32[]{:S(2)}) collective-permute-start(bf16[256,768]{1,0:T(8,128)(2,1)S(1)} %get-tuple-element.40), channel_id=1, source_target_pairs={{2,0},{4,2},{6,4},{7,6},{5,7},{3,5},{1,3},{0,1},{10,8},{12,10},{14... | collective-permute-start | bytes 1179656 | tf_op jit(solution)/shard_map/ppermute | solution.py:213
  112.4 9.5 %collective-permute-start.8 = (bf16[256,768]{1,0:T(8,128)(2,1)S(1)}, bf16[256,768]{1,0:T(8,128)(2,1)S(1)}, u32[]{:S(2)}, u32[]{:S(2)}) collective-permute-start(bf16[256,768]{1,0:T(8,128)(2,1)S(1)} %get-tuple-element.36), channel_id=1, source_target_pairs={{0,2},{2,4},{4,6},{6,7},{7,5},{5,3},{3,1},{1,0},{8,10},{10,12},{12... | collective-permute-start | bytes 1179656 | tf_op jit(solution)/shard_map/ppermute | solution.py:210
  113.3 17.5 %collective-permute-start.13 = (bf16[512,768]{1,0:T(8,128)(2,1)S(1)}, bf16[512,768]{1,0:T(8,128)(2,1)S(1)}, u32[]{:S(2)}, u32[]{:S(2)}) collective-permute-start(bf16[512,768]{1,0:T(8,128)(2,1)S(1)} %pad_maximum_fusion.1), channel_id=1, source_target_pairs={{2,0},{4,2},{6,4},{7,6},{5,7},{3,5},{1,3},{0,1},{10,8},{12,10},{14... | collective-permute-start | bytes 2359304 | tf_op jit(solution)/shard_map/ppermute | solution.py:213
  122.0 17.5 %collective-permute-start.9 = (bf16[512,768]{1,0:T(8,128)(2,1)S(1)}, bf16[512,768]{1,0:T(8,128)(2,1)S(1)}, u32[]{:S(2)}, u32[]{:S(2)}) collective-permute-start(bf16[512,768]{1,0:T(8,128)(2,1)S(1)} %pad_maximum_fusion), channel_id=1, source_target_pairs={{0,2},{2,4},{4,6},{6,7},{7,5},{5,3},{3,1},{1,0},{8,10},{10,12},{12... | collective-permute-start | bytes 2359304 | tf_op jit(solution)/shard_map/ppermute | solution.py:210
  131.0 16.5 %collective-permute-start.14 = (bf16[512,768]{1,0:T(8,128)(2,1)S(1)}, bf16[512,768]{1,0:T(8,128)(2,1)S(1)}, u32[]{:S(2)}, u32[]{:S(2)}) collective-permute-start(bf16[512,768]{1,0:T(8,128)(2,1)S(1)} %add_convert_fusion.1), channel_id=1, source_target_pairs={{2,0},{4,2},{6,4},{7,6},{5,7},{3,5},{1,3},{0,1},{10,8},{12,10},{14... | collective-permute-start | bytes 2359304 | tf_op jit(solution)/shard_map/ppermute | solution.py:213
  139.8 16.5 %collective-permute-start.10 = (bf16[512,768]{1,0:T(8,128)(2,1)S(1)}, bf16[512,768]{1,0:T(8,128)(2,1)S(1)}, u32[]{:S(2)}, u32[]{:S(2)}) collective-permute-start(bf16[512,768]{1,0:T(8,128)(2,1)S(1)} %add_convert_fusion.3), channel_id=1, source_target_pairs={{0,2},{2,4},{4,6},{6,7},{7,5},{5,3},{3,1},{1,0},{8,10},{10,12},{12... | collective-permute-start | bytes 2359304 | tf_op jit(solution)/shard_map/ppermute | solution.py:210
  148.5 14.9 %collective-permute-start.15 = (bf16[512,768]{1,0:T(8,128)(2,1)}, bf16[512,768]{1,0:T(8,128)(2,1)S(1)}, u32[]{:S(2)}, u32[]{:S(2)}) collective-permute-start(bf16[512,768]{1,0:T(8,128)(2,1)} %add_convert_fusion), channel_id=1, source_target_pairs={{2,0},{4,2},{6,4},{7,6},{5,7},{3,5},{1,3},{0,1},{10,8},{12,10},{14... | collective-permute-start | bytes 2359304 | tf_op jit(solution)/shard_map/ppermute | solution.py:213
  156.3 1.3 copy-start.4
  156.3 1.3 copy-start.5
  157.3 13.6 %collective-permute-start.11 = (bf16[512,768]{1,0:T(8,128)(2,1)}, bf16[512,768]{1,0:T(8,128)(2,1)}, u32[]{:S(2)}, u32[]{:S(2)}) collective-permute-start(bf16[512,768]{1,0:T(8,128)(2,1)} %add_convert_fusion.2), channel_id=1, source_target_pairs={{0,2},{2,4},{4,6},{6,7},{7,5},{5,3},{3,1},{1,0},{8,10},{10,12},{12... | collective-permute-start | bytes 2359304 | tf_op jit(solution)/shard_map/ppermute | solution.py:210
